TPU v7x, 32 devices: a whole 2x2x4 slice. The times are simulated.
32 devices in a mesh: rep: 8 (over y, x, core), grp: 4 (over z).
Axes of the slice: x: 2, y: 2, z: 4, core: 2. Of those that a mesh axis runs over, the one named last changes fastest.
Arguments:
- tokens: bfloat16 [4096, 1536], P(('rep', 'grp')), may hold values from -6 to 6
- attn_gain: bfloat16 [1536], P('grp'), may hold values from 0.5 to 1.5
- query_key_value_weight: bfloat16 [1536, 2560], P('grp'), may hold values from -0.15625 to 0.15625
- attn_proj: bfloat16 [1536, 1536], P('grp'), may hold values from -1.25 to 1.25
- mlp_gain: bfloat16 [1536], P('grp'), may hold values from 0.5 to 1.5
- w_router: bfloat16 [1536, 16], P('grp'), may hold values from -0.078125 to 0.078125
- w_gate_up: bfloat16 [1536, 16, 1024], P('grp'), may hold values from -0.15625 to 0.15625
- w_down: bfloat16 [1536, 16, 512], P('grp'), may hold values from -1 to 1
- prefix_len: int32 [32], P(('rep', 'grp')), may hold values from 0 to 128
- expert_ids: int32 [4096, 8], P(('rep', 'grp')), may hold values from 0 to 15, all different within a row
- priority: int32 [32, 1024], P(('rep', 'grp')), may hold values from 0 to 1023, each once within a row
- cotangent: bfloat16 [4096, 1536], P(('rep', 'grp')), may hold values from -6 to 6
Outputs:
- output: bfloat16 [4096, 1536], P(('rep', 'grp'))
- grad_tokens: float32 [4096, 1536], P(('rep', 'grp'))
- grad_attn_gain: float32 [1536], P('grp')
- grad_w_qkv: float32 [1536, 2560], P('grp')
- grad_attn_proj: float32 [1536, 1536], P('grp')
- grad_mlp_gain: float32 [1536], P('grp')
- grad_w_router: float32 [1536, 16], P('grp')
- grad_w_gate_up: float32 [1536, 16, 1024], P('grp')
- grad_w_down: float32 [1536, 16, 512], P('grp')
Inputs may be any that keep to these rules, and one draw needn't show every extreme that they name: `prefix_len`: positions below a sequence's prefix length attend to one another in both directions. `expert_ids`: the 8 experts of a token are different. `priority`: each row holds every number of 0 to 1023 once.
All inputs are finite; a program needn't handle non-finite values.
Results may differ from a plain program's by a relative error of at most 0.015.
Values may be sent and summed in bfloat16 or wider, within the bound.
A program may use at most 576 MiB of HBM per device.

v0:
```python
import jax
import jax.numpy as jnp
from jax import lax
from jax.sharding import PartitionSpec as P

QUERY_HEADS = 24
KEY_VALUE_HEADS = 8
HEAD_WIDTH = 64
HID = 512
EXPERTS = 16
CAP = 72
EPS = 1e-05
BF = jnp.bfloat16
F32 = jnp.float32
QPK = QUERY_HEADS // KEY_VALUE_HEADS
BIG = 1 << 20


def dot(a, b):
    return jnp.dot(a, b, preferred_element_type=F32)


def rope_tables(length):
    half = HEAD_WIDTH // 2
    position = jnp.arange(length, dtype=F32)[:, None]
    inverse_freq = 10000.0 ** (-jnp.arange(half, dtype=F32) * 2.0 / HEAD_WIDTH)
    angles = position * inverse_freq[None, :]
    return (jnp.cos(angles), jnp.sin(angles))


def rotate(v, cos, sin):
    half = HEAD_WIDTH // 2
    a, b = (v[..., :half], v[..., half:])
    return jnp.concatenate([a * cos - b * sin, b * cos + a * sin], axis=-1)


def routing(expert_ids, priority, logits):
    seq, top = expert_ids.shape
    choose = expert_ids[:, :, None] == jnp.arange(EXPERTS, dtype=jnp.int32)[None, None, :]
    chosen = jnp.any(choose, axis=1)
    rank_of = jnp.sum(jnp.where(choose, priority.reshape(seq, top)[:, :, None], 0), axis=1)
    rank_of = jnp.where(chosen, rank_of, BIG)
    slot = jnp.sum((rank_of[None, :, :] < rank_of[:, None, :]).astype(jnp.int32), axis=1)
    kept = chosen & (slot < CAP)
    top_logit = jnp.max(jnp.where(chosen, logits, -jnp.inf), axis=1, keepdims=True)
    gate_exp = jnp.where(chosen, jnp.exp(jnp.where(chosen, logits - top_logit, 0.0)), 0.0)
    gates = gate_exp / jnp.sum(gate_exp, axis=1, keepdims=True)
    return (gates, kept)


def shards(
    reps,
    grps,
    tokens,
    attn_gain,
    query_key_value_weight,
    attn_proj,
    mlp_gain,
    w_router,
    w_gate_up,
    w_down,
    prefix_len,
    expert_ids,
    priority,
    cotangent,
):
    seq, width = tokens.shape
    own = width // grps
    local_experts = EXPERTS // grps
    heads = KEY_VALUE_HEADS
    groups = None if reps == heads else [list(range(i, i + heads)) for i in range(0, reps, heads)]
    rep, grp = (lax.axis_index("rep"), lax.axis_index("grp"))
    head = lax.rem(rep, heads)
    qw, hw = (QPK * HEAD_WIDTH, HEAD_WIDTH)
    q_all = QUERY_HEADS * HEAD_WIDTH
    small = jnp.concatenate([attn_gain[:, None], mlp_gain[:, None], w_router], axis=1)
    small = lax.all_gather(small, "grp", axis=0, tiled=True)
    gain_one, gain_two = (small[:, 0].astype(F32)[None, :], small[:, 1].astype(F32)[None, :])
    router = small[:, 2:]
    qkv_cols = jnp.concatenate(
        [
            lax.dynamic_slice_in_dim(query_key_value_weight, head * qw, qw, 1),
            lax.dynamic_slice_in_dim(query_key_value_weight, q_all + head * hw, hw, 1),
            lax.dynamic_slice_in_dim(query_key_value_weight, q_all + heads * hw + head * hw, hw, 1),
        ],
        axis=1,
    )
    qkv_head = lax.all_gather(qkv_cols, "grp", axis=0, tiled=True)
    row = head * qw + jnp.arange(qw)
    mine = row // own == grp
    proj_rows = jnp.where(
        mine[:, None], jnp.take(attn_proj, jnp.where(mine, row - grp * own, 0), axis=0), 0
    )
    proj_head = lax.psum(proj_rows, "grp")
    piece = own // reps
    gu_piece = lax.dynamic_slice_in_dim(w_gate_up, rep * piece, piece, 0)
    dn_piece = lax.dynamic_slice_in_dim(w_down, rep * piece, piece, 0)
    both = jnp.concatenate([gu_piece, dn_piece], axis=2)
    both = both.reshape(piece, grps, local_experts, 3 * HID).transpose(1, 2, 0, 3)
    both = lax.all_to_all(both, "grp", 0, 0, tiled=True)
    both = lax.all_gather(both, "rep", axis=0, tiled=False)
    both = both.transpose(2, 1, 0, 3, 4).reshape(local_experts, width, 3 * HID)
    wgu, wdn = (both[:, :, : 2 * HID], both[:, :, 2 * HID :])
    tokens_f = tokens.astype(F32)
    inverse_one = lax.rsqrt(jnp.mean(tokens_f * tokens_f, axis=1, keepdims=True) + EPS)
    normed_one = tokens_f * inverse_one
    act_one = (normed_one * gain_one).astype(BF)
    act_plane = lax.all_gather(act_one, "rep", axis=0, tiled=True, axis_index_groups=groups)
    prefix_plane = lax.all_gather(prefix_len, "rep", axis=0, tiled=True, axis_index_groups=groups)
    cos, sin = rope_tables(seq)
    projected = dot(act_plane, qkv_head).reshape(heads, seq, QPK + 2, HEAD_WIDTH)
    cos_b, sin_b = (cos[None, :, None, :], sin[None, :, None, :])
    turned = rotate(projected[:, :, : QPK + 1], cos_b, sin_b).astype(BF)
    query = turned[:, :, :QPK]
    key = turned[:, :, QPK]
    value = projected[:, :, QPK + 1].astype(BF)
    scale = HEAD_WIDTH ** (-0.5)
    row_pos, col_pos = (jnp.arange(seq)[:, None], jnp.arange(seq)[None, :])
    allowed = (col_pos <= row_pos)[None] | (col_pos[None] < prefix_plane[:, None, None])
    scores = jnp.einsum("bsgd,btd->bgst", query, key, preferred_element_type=F32) * scale
    scores = jnp.where(allowed[:, None], scores, -1e30)
    exps = jnp.exp(scores - jnp.max(scores, axis=-1, keepdims=True))
    probs = exps / jnp.sum(exps, axis=-1, keepdims=True)
    probs_low = probs.astype(BF)
    attended = jnp.einsum("bgst,btd->bsgd", probs_low, value, preferred_element_type=F32)
    attended = attended.astype(BF).reshape(heads * seq, qw)
    part = dot(attended, proj_head).astype(BF)
    part = lax.psum_scatter(part, "rep", scatter_dimension=0, tiled=True, axis_index_groups=groups)
    residual = tokens_f + part.astype(F32)
    inverse_two = lax.rsqrt(jnp.mean(residual * residual, axis=1, keepdims=True) + EPS)
    normed_two = residual * inverse_two
    act_two = (normed_two * gain_two).astype(BF)
    gates, kept = routing(expert_ids, priority, dot(act_two, router))
    dy_all = lax.all_gather(cotangent, "grp", axis=0, tiled=True)
    x_all = lax.all_gather(act_two, "grp", axis=0, tiled=True)
    weight = lax.all_gather(jnp.where(kept, gates, 0.0), "grp", axis=0, tiled=True)
    weight = lax.dynamic_slice_in_dim(weight, grp * local_experts, local_experts, 1).T[:, :, None]
    gate_up = jnp.einsum("td,edh->eth", x_all, wgu, preferred_element_type=F32)
    g, u = (gate_up[..., :HID], gate_up[..., HID:])
    sig = jax.nn.sigmoid(g)
    silu = g * sig
    hidden = silu * u
    hidden_w = (hidden * weight).astype(BF)
    back = jnp.einsum("td,edh->eth", dy_all, wdn, preferred_element_type=F32)
    grad_gate_part = jnp.sum(back * hidden, axis=2)
    grad_hidden = back * weight
    ggu = jnp.concatenate(
        [grad_hidden * u * sig * (1.0 + g * (1.0 - sig)), grad_hidden * silu], axis=2
    ).astype(BF)
    out_part = jnp.einsum("eth,edh->td", hidden_w, wdn, preferred_element_type=F32).astype(BF)
    gact_part = jnp.einsum("eth,edh->td", ggu, wgu, preferred_element_type=F32).astype(BF)
    gact = lax.psum_scatter(gact_part, "grp", scatter_dimension=0, tiled=True).astype(F32)
    grad_gates = lax.all_to_all(grad_gate_part.T, "grp", 0, 1, tiled=True)
    grad_gates = jnp.where(kept, grad_gates, 0.0)
    gw_gu = jnp.einsum("td,eth->edh", x_all, ggu, preferred_element_type=F32).astype(BF)
    gw_dn = jnp.einsum("td,eth->edh", dy_all, hidden_w, preferred_element_type=F32).astype(BF)
    gw = jnp.concatenate([gw_gu, gw_dn], axis=2)
    gw = gw.reshape(local_experts, grps, reps, piece, 3 * HID).transpose(2, 1, 3, 0, 4)
    gw = gw.reshape(reps * grps * piece, EXPERTS // grps * 3 * HID)
    gw = lax.psum_scatter(gw, "rep", scatter_dimension=0, tiled=True)
    gw = gw.reshape(grps, piece, local_experts, 3 * HID)
    gw = lax.all_to_all(gw, "grp", 0, 0, tiled=True)
    gw = gw.transpose(1, 0, 2, 3).reshape(piece, EXPERTS, 3 * HID)
    gw = lax.all_gather(gw, "rep", axis=0, tiled=True)
    grad_gu = gw[:, :, : 2 * HID].astype(F32)
    grad_dn = gw[:, :, 2 * HID :].astype(F32)
    out = lax.psum_scatter(out_part, "grp", scatter_dimension=0, tiled=True).astype(F32)
    output = (residual + out).astype(BF)
    grad_logits = (
        gates * (grad_gates - jnp.sum(gates * grad_gates, axis=1, keepdims=True))
    ).astype(BF)
    gact = gact + dot(grad_logits, router.T)
    router_term = dot(act_two.T, grad_logits)
    gain_two_term = jnp.sum(gact * normed_two, axis=0)
    scaled = gact * gain_two
    dy = cotangent.astype(F32)
    grad_residual = dy + inverse_two * (
        scaled - normed_two * jnp.mean(scaled * normed_two, axis=1, keepdims=True)
    )
    gres_low = grad_residual.astype(BF)
    gres_plane = lax.all_gather(gres_low, "rep", axis=0, tiled=True, axis_index_groups=groups)
    proj_term = dot(attended.T, gres_plane)
    grad_att = dot(gres_plane, proj_head.T).astype(BF).reshape(heads, seq, QPK, HEAD_WIDTH)
    grad_value = jnp.einsum("bgst,bsgd->btd", probs_low, grad_att, preferred_element_type=F32)
    grad_probs = jnp.einsum("bsgd,btd->bgst", grad_att, value, preferred_element_type=F32)
    grad_scores = (
        probs * (grad_probs - jnp.sum(probs * grad_probs, axis=-1, keepdims=True))
    ).astype(BF)
    grad_query = jnp.einsum("bgst,btd->bsgd", grad_scores, key, preferred_element_type=F32) * scale
    grad_key = jnp.einsum("bgst,bsgd->btd", grad_scores, query, preferred_element_type=F32) * scale
    turned_back = rotate(jnp.concatenate([grad_query, grad_key[:, :, None]], axis=2), cos_b, -sin_b)
    gproj = jnp.concatenate([turned_back, grad_value[:, :, None]], axis=2).astype(BF)
    gproj = gproj.reshape(heads * seq, qw + 2 * hw)
    qkv_term = dot(act_plane.T, gproj)
    gact_one = dot(gproj, qkv_head.T).astype(BF)
    gact_one = lax.psum_scatter(
        gact_one, "rep", scatter_dimension=0, tiled=True, axis_index_groups=groups
    ).astype(F32)
    gain_one_term = jnp.sum(gact_one * normed_one, axis=0)
    scaled_one = gact_one * gain_one
    grad_tokens = grad_residual + inverse_one * (
        scaled_one - normed_one * jnp.mean(scaled_one * normed_one, axis=1, keepdims=True)
    )
    qkv_own = lax.psum_scatter(qkv_term.astype(BF), "grp", scatter_dimension=0, tiled=True)
    proj_sum = lax.psum(proj_term.astype(BF), "grp")
    if groups is not None:
        across = [[i + heads * j for j in range(reps // heads)] for i in range(heads)]
        qkv_own = lax.psum(qkv_own, "rep", axis_index_groups=across)
        proj_sum = lax.psum(proj_sum, "rep", axis_index_groups=across)
    qkv_own = lax.all_gather(qkv_own, "rep", axis=0, tiled=False, axis_index_groups=groups)
    qkv_own = qkv_own.astype(F32)
    grad_qkv = jnp.concatenate(
        [
            qkv_own[:, :, lo:hi].transpose(1, 0, 2).reshape(own, -1)
            for lo, hi in ((0, qw), (qw, qw + hw), (qw + hw, qw + 2 * hw))
        ],
        axis=1,
    )
    proj_all = lax.all_gather(proj_sum, "rep", axis=0, tiled=True, axis_index_groups=groups)
    grad_proj = lax.dynamic_slice_in_dim(proj_all, grp * own, own, 0).astype(F32)
    terms = jnp.concatenate([gain_one_term[:, None], gain_two_term[:, None], router_term], axis=1)
    terms = lax.psum(lax.psum_scatter(terms, "grp", scatter_dimension=0, tiled=True), "rep")
    return (
        output,
        grad_tokens,
        terms[:, 0],
        grad_qkv,
        grad_proj,
        terms[:, 1],
        terms[:, 2:],
        grad_gu,
        grad_dn,
    )


def solution(mesh):
    tok, par = (("rep", "grp"), "grp")
    in_specs = (
        P(tok, None),
        P(par),
        P(par, None),
        P(par, None),
        P(par),
        P(par, None),
        P(par, None, None),
        P(par, None, None),
        P(tok),
        P(tok, None),
        P(tok, None),
        P(tok, None),
    )
    out_specs = (
        P(tok, None),
        P(tok, None),
        P(par),
        P(par, None),
        P(par, None),
        P(par),
        P(par, None),
        P(par, None, None),
        P(par, None, None),
    )
    reps, grps = (mesh.shape["rep"], mesh.shape["grp"])

    def body(*args):
        return shards(reps, grps, *args)

    return jax.shard_map(body, mesh=mesh, in_specs=in_specs, out_specs=out_specs, check_vma=False)
```

profile of v0, /device:TPU:0, one launch (start us, length us, event | category | flops | bytes accessed | tf_op | source)
XLA Modules:
  0.0 1020.9 jit_solution(18360861975439800956)
XLA Ops:
  8.1 1.2 fusion.53
  11.4 14.9 %all_gather.42 = bf16[1536,18]{0,1:T(8,128)(2,1)S(1)} all-gather(bf16[384,18]{0,1:T(8,128)(2,1)S(1)} %pad_maximum_fusion.17), channel_id=1, replica_groups=mesh['rep'=8,'grp'=4] {'grp'}, dimensions={0}, use_global_device_ids=true | all-gather | bytes 69120 | tf_op jit(solution)/shard_map/all_gather | solution.py:77
  26.3 1.9 fusion.50
  32.6 8.0 all-reduce
  43.2 30.3 %all_gather.44 = bf16[1536,320]{1,0:T(8,128)(2,1)S(1)} all-gather(bf16[384,320]{1,0:T(8,128)(2,1)S(1)} %pad_maximum_fusion.9), channel_id=1, replica_groups=mesh['rep'=8,'grp'=4] {'grp'}, dimensions={0}, use_global_device_ids=true | all-gather | bytes 1228800 | tf_op jit(solution)/shard_map/all_gather | solution.py:88
  73.8 3.1 convolution_bitcast_fusion
  77.5 1.9 fusion.104
  79.4 1.7 fusion.38
  81.4 3.7 convolution_convert_fusion.1
  86.4 1.5 constant_dynamic-slice_fusion.1
  88.2 1.3 copy.159
  89.5 56.0 %all_to_all.29 = bf16[4,4,48,1536]{3,2,1,0:T(8,128)(2,1)} all-to-all(bf16[4,4,48,1536]{3,2,1,0:T(8,128)(2,1)S(1)} %bitcast.193), channel_id=1, replica_groups=mesh['rep'=8,'grp'=4] {'grp'}, dimensions={0} | all-to-all | bytes 4718592 | tf_op jit(solution)/shard_map/all_to_all | solution.py:100
  146.8 1.9 multiply_convert_fusion.3
  150.9 2.5 convert_reduce_fusion
  153.4 1.3 select_reduce_fusion.1
  154.7 88.9 %all-gather.23.cloned.1.call-done = bf16[32,4,48,1536]{3,2,1,0:T(8,128)(2,1)} async-done(((bf16[4,4,48,1536]{3,2,1,0:T(8,128)(2,1)}), bf16[32,4,48,1536]{3,2,1,0:T(8,128)(2,1)}) %all-gather.23.cloned.1.call-update) | async-done | bytes 18874384 | tf_op jit(solution)/shard_map/all_gather | solution.py:101
  243.6 17.1 %copy.160 = bf16[4,4,8,48,1536]{4,3,2,1,0:T(8,128)(2,1)} copy(bf16[4,4,8,48,1536]{4,3,0,1,2:T(8,128)(2,1)} %bitcast.188) | data formatting | bytes 37748736 | tf_op jit(solution)/shard_map/transpose | solution.py:102
  260.8 22.1 %all-gather.13.cloned.1.call-done = bf16[512,1536]{1,0:T(8,128)(2,1)} async-done(((bf16[128,1536]{1,0:T(8,128)(2,1)}), bf16[512,1536]{1,0:T(8,128)(2,1)}) %all-gather.13.cloned.1.call-update) | async-done | bytes 1572880 | tf_op jit(solution)/shard_map/all_gather | solution.py:135
  282.8 12.3 %fusion.18 = f32[4,512,1024]{1,2,0:T(8,128)} fusion(bf16[4,1536,1536]{2,1,0:T(8,128)(2,1)} %bitcast.184, bf16[512,1536]{1,0:T(8,128)(2,1)} %all-gather.13.cloned.1.call-done), kind=kOutput, calls=%fused_computation.31 | convolution fusion | flops 6442450944 | bytes 22544384 | tf_op jit(solution)/shard_map/td,edh->eth/dot_general | solution.py:138
  295.2 25.2 %all-gather.15.cloned.1.call-done = bf16[512,1536]{1,0:T(8,128)(2,1)} async-done(((bf16[128,1536]{1,0:T(8,128)(2,1)}), bf16[512,1536]{1,0:T(8,128)(2,1)}) %all-gather.15.cloned.1.call-update) | async-done | bytes 1572880 | tf_op jit(solution)/shard_map/all_gather | solution.py:134
  320.3 12.6 %fusion.10 = (f32[4,512]{1,0:T(4,128)}, f32[4,512,512]{2,1,0:T(8,128)}) fusion(f32[4,512,1024]{1,2,0:T(8,128)} %fusion.18, bf16[512,1536]{1,0:T(8,128)(2,1)} %all-gather.15.cloned.1.call-done, bf16[4,1536,1536]{2,1,0:T(8,128)(2,1)} %bitcast.185), kind=kOutput, calls=%fused_computation.19 | convolution fusion | flops 3228563456 | bytes 20455424 | tf_op jit(solution)/shard_map/td,edh->eth/dot_general | solution.py:144
  332.9 3.2 all-to-all-start.1
  336.2 5.5 all-to-all-done.1
  341.8 13.5 %all_gather.49 = f32[512,16]{0,1:T(8,128)S(1)} all-gather(f32[128,16]{0,1:T(8,128)S(1)} %get-tuple-element.80), channel_id=1, replica_groups=mesh['rep'=8,'grp'=4] {'grp'}, dimensions={0}, use_global_device_ids=true | all-gather | bytes 40960 | tf_op jit(solution)/shard_map/all_gather | solution.py:136
  355.3 6.9 multiply_convert_fusion.1
  362.2 1.4 copy-done.12
  364.2 10.8 %fusion.24 = bf16[512,1536]{1,0:T(8,128)(2,1)} fusion(bf16[4,1536,1536]{2,1,0:T(8,128)(2,1)} %bitcast.186, bf16[4,512,512]{1,2,0:T(8,128)(2,1)S(1)} %get-tuple-element.65, bf16[4,512,512]{1,2,0:T(8,128)(2,1)S(1)} %get-tuple-element.64), kind=kOutput, calls=%fused_computation.33 | convolution fusion | flops 6451625984 | bytes 18350080 | tf_op jit(solution)/shard_map/eth,edh->td/dot_general | solution.py:151
  375.1 33.6 %reduce-scatter.14.cloned.1.call-done = bf16[128,1536]{1,0:T(8,128)(2,1)} async-done(((bf16[512,1536]{1,0:T(8,128)(2,1)}), bf16[128,1536]{1,0:T(8,128)(2,1)}) %reduce-scatter.14.cloned.1.call-update) | async-done | bytes 393232 | tf_op jit(solution)/shard_map/reduce_scatter | solution.py:152
  408.7 1.5 multiply_reduce_fusion
  412.3 31.3 %all-gather.17.cloned.1.call-done = bf16[1024,1536]{1,0:T(8,128)(2,1)} async-done(((bf16[128,1536]{1,0:T(8,128)(2,1)}), bf16[1024,1536]{1,0:T(8,128)(2,1)}) %all-gather.17.cloned.1.call-update) | async-done | bytes 3145744 | tf_op jit(solution)/shard_map/all_gather | solution.py:181
  443.6 3.2 fusion.37
  446.9 2.0 fusion.46
  451.2 3.5 convolution_convert_fusion.2
  454.8 4.1 convolution_convert_fusion.3
  458.8 2.5 copy.196
  461.6 7.0 convert_bitcast_fusion
  468.6 10.6 %fusion.5 = bf16[4,1536,1024]{1,2,0:T(8,128)(2,1)} fusion(bf16[4,512,512]{1,2,0:T(8,128)(2,1)S(1)} %copy-done.15, bf16[4,512,512]{1,2,0:T(8,128)(2,1)S(1)} %copy-done.13, bf16[512,1536]{1,0:T(8,128)(2,1)S(1)} %copy-done.34), kind=kOutput, calls=%fused_computation.9 | convolution fusion | flops 6457131008 | bytes 18350080 | tf_op jit(solution)/shard_map/td,eth->edh/dot_general | solution.py:155
  479.2 1.6 convolution_convert_fusion.4
  480.9 20.9 %pad_maximum_fusion = bf16[4,1536,1536]{1,2,0:T(8,128)(2,1)} fusion(bf16[4,1536,512]{1,2,0:T(8,128)(2,1)} %convert_bitcast_fusion, bf16[4,1536,1024]{1,2,0:T(8,128)(2,1)} %fusion.5), kind=kLoop, calls=%fused_computation.2 | loop fusion | flops 37748736 | bytes 37748736 | tf_op jit(solution)/shard_map/concatenate | solution.py:157
  501.8 24.7 %copy.178 = bf16[4,1536,1536]{2,1,0:T(8,128)(2,1)} copy(bf16[4,1536,1536]{1,2,0:T(8,128)(2,1)} %pad_maximum_fusion) | data formatting | bytes 37748736 | tf_op jit(solution)/shard_map/concatenate | solution.py:157
  526.5 21.6 %copy.179 = bf16[8,4,48,4,1536]{4,3,2,1,0:T(4,128)(2,1)S(1)} copy(bf16[8,4,48,4,1536]{4,2,0,1,3:T(8,128)(2,1)} %bitcast.182) | data formatting | bytes 37748736 | tf_op jit(solution)/shard_map/transpose | solution.py:158
  548.1 9.7 copy.207
  557.9 1.5 copy-done.11
  559.4 7.4 fusion.21
  567.1 1.9 fusion.52
  569.8 1.8 copy.197
  572.7 111.4 %reduce-scatter.20.cloned.1.call-done = bf16[192,6144]{1,0:T(8,128)(2,1)} async-done(((bf16[1536,6144]{1,0:T(8,128)(2,1)}), bf16[192,6144]{1,0:T(8,128)(2,1)}) %reduce-scatter.20.cloned.1.call-update) | async-done | bytes 2359312 | tf_op jit(solution)/shard_map/reduce_scatter | solution.py:160
  684.1 3.5 reshape.284
  687.7 84.3 %all_to_all.30 = bf16[4,48,4,1536]{3,2,1,0:T(4,128)(2,1)S(1)} all-to-all(bf16[4,48,4,1536]{3,2,1,0:T(4,128)(2,1)S(1)} %reshape.284), channel_id=1, replica_groups=mesh['rep'=8,'grp'=4] {'grp'}, dimensions={0} | all-to-all | bytes 4718592 | tf_op jit(solution)/shard_map/all_to_all | solution.py:162
  772.0 1.9 copy.180
  774.0 2.6 fusion.49
  776.5 3.4 reduce-scatter.18.cloned.1.call-done
  780.0 23.5 %psum.22 = f32[384,18]{0,1:T(8,128)S(1)} all-reduce(f32[384,18]{0,1:T(8,128)} %reduce-scatter.18.cloned.1.call-done), channel_id=1, replica_groups=mesh['rep'=8,'grp'=4] {'rep'}, use_global_device_ids=true, to_apply=%region_22.23 | all-reduce | flops 6912 | bytes 55296 | tf_op jit(solution)/shard_map/psum | solution.py:222
  804.7 3.8 all-gather.25.cloned.1.call-done
  808.5 2.0 convert_element_type.169
  812.3 2.2 pad_maximum_fusion.2
  814.5 5.5 copy.181
  820.0 29.4 %all-gather.19.cloned.1.call-done = bf16[1536,1536]{1,0:T(8,128)(2,1)} async-done(((bf16[192,1536]{1,0:T(8,128)(2,1)}), bf16[1536,1536]{1,0:T(8,128)(2,1)}) %all-gather.19.cloned.1.call-update) | async-done | bytes 4718608 | tf_op jit(solution)/shard_map/all_gather | solution.py:219
  849.4 3.0 dynamic-slice_convert_fusion
  852.4 98.3 %all-gather.21.cloned.1.call-done = bf16[384,16,1536]{2,0,1:T(8,128)(2,1)} async-done(((bf16[48,16,1536]{2,0,1:T(8,128)(2,1)}), bf16[384,16,1536]{2,0,1:T(8,128)(2,1)}) %all-gather.21.cloned.1.call-update) | async-done | bytes 18874384 | tf_op jit(solution)/shard_map/all_gather | solution.py:164
  950.7 9.3 slice_convert_fusion.1
  960.0 16.6 %copy.183 = f32[384,16,512]{2,1,0:T(8,128)} copy(f32[384,16,512]{2,0,1:T(8,128)} %slice_convert_fusion.1) | data formatting | bytes 25165824
  976.6 7.4 slice_convert_fusion
  984.0 29.1 %copy.182 = f32[384,16,1024]{2,1,0:T(8,128)} copy(f32[384,16,1024]{2,0,1:T(8,128)S(1)} %slice_convert_fusion) | data formatting | bytes 50331648
  (177 shorter events, 24.9 us)
Async XLA Ops:
  8.0 20.4 %copy-start = (bf16[384,1536]{1,0:T(8,128)(2,1)S(1)}, bf16[384,1536]{1,0:T(8,128)(2,1)}, u32[]{:S(2)}) copy-start(bf16[384,1536]{1,0:T(8,128)(2,1)} %param.15) | copy-start | bytes 3538948
  8.0 65.7 %all-gather.11.cloned.1.call-start = ((), (), s32[]{:S(2)}) async-start(), calls=%async_computation.10 | async-start | bytes 3538944 | tf_op jit(solution)/shard_map/all_gather | solution.py:108
  9.3 19.0 %copy-start.27 = (f32[128]{0:T(128)}, f32[128]{0:T(128)S(1)}, u32[]{:S(2)}) copy-start(f32[128]{0:T(128)S(1)} %add_rsqrt_fusion.1) | copy-start | bytes 1540
  26.3 3.2 copy-start.18
  28.3 53.1 %all-reduce.4.cloned.1.call-start = ((), (), s32[]{:S(2)}) async-start(), calls=%async_computation.11 | async-start | bytes 1179648 | tf_op jit(solution)/shard_map/psum | solution.py:94
  28.4 2.9 copy-start.35
  30.5 115.1 %reduce-scatter.10.cloned.1.call-start = ((), (), s32[]{:S(2)}) async-start(), calls=%async_computation.12 | async-start | bytes 3538944 | tf_op jit(solution)/shard_map/reduce_scatter | solution.py:128
  77.5 3.6 copy-start.20
  79.4 2.0 copy-start.22
  85.2 158.5 %all-gather.23.cloned.1.call-start = ((), (), s32[]{:S(2)}) async-start(), calls=%async_computation.24 | async-start | bytes 21233664 | tf_op jit(solution)/shard_map/all_gather | solution.py:101
  89.5 56.1 %copy-start.2 = (bf16[128,1536]{1,0:T(8,128)(2,1)S(1)}, bf16[128,1536]{1,0:T(8,128)(2,1)}, u32[]{:S(2)}) copy-start(bf16[128,1536]{1,0:T(8,128)(2,1)} %param.12) | copy-start | bytes 1179652
  145.5 3.9 copy-start.24
  145.5 4.4 copy-start.30
  145.5 137.3 %all-gather.13.cloned.1.call-start = ((), (), s32[]{:S(2)}) async-start(), calls=%async_computation.13 | async-start | bytes 1966080 | tf_op jit(solution)/shard_map/all_gather | solution.py:135
  146.8 263.4 %copy-start.25 = (f32[128]{0:T(128)}, f32[128]{0:T(128)S(1)}, u32[]{:S(2)}) copy-start(f32[128]{0:T(128)S(1)} %add_rsqrt_fusion) | copy-start | bytes 1540
  148.8 171.5 %all-gather.15.cloned.1.call-start = ((), (), s32[]{:S(2)}) async-start(), calls=%async_computation.15 | async-start | bytes 1966080 | tf_op jit(solution)/shard_map/all_gather | solution.py:134
  332.9 8.8 all-to-all-start.1
  336.1 72.6 %reduce-scatter.14.cloned.1.call-start = ((), (), s32[]{:S(2)}) async-start(), calls=%async_computation.16 | async-start | bytes 1966080 | tf_op jit(solution)/shard_map/reduce_scatter | solution.py:152
  362.2 1.4 copy-start.12
  362.2 2.0 copy-start.14
  364.2 44.5 %copy-start.3 = (bf16[128,1536]{1,0:T(8,128)(2,1)S(1)}, bf16[128,1536]{1,0:T(8,128)(2,1)}, u32[]{:S(2)}) copy-start(bf16[128,1536]{1,0:T(8,128)(2,1)} %reduce-scatter.10.cloned.1.call-done) | copy-start | bytes 1179652
  375.1 36.0 %copy-start.7 = (bf16[128,1536]{1,0:T(8,128)(2,1)S(1)}, bf16[128,1536]{1,0:T(8,128)(2,1)}, u32[]{:S(2)}) copy-start(bf16[128,1536]{1,0:T(8,128)(2,1)} %param.23) | copy-start | bytes 1179652
  375.1 68.5 %all-gather.17.cloned.1.call-start = ((), (), s32[]{:S(2)}) async-start(), calls=%async_computation.17 | async-start | bytes 3538944 | tf_op jit(solution)/shard_map/all_gather | solution.py:181
  410.2 0.9 copy-start.4
  410.2 36.5 %copy-start.31 = (f32[128]{0:T(128)}, f32[128]{0:T(128)S(1)}, u32[]{:S(2)}) copy-start(f32[128]{0:T(128)S(1)} %broadcast_multiply_fusion.1) | copy-start | bytes 1540
  412.2 34.6 %copy-start.23 = (f32[8,3,128]{2,1,0:T(4,128)S(1)}, f32[8,3,128]{2,1,0:T(4,128)}, u32[]{:S(2)}) copy-start(f32[8,3,128]{2,1,0:T(4,128)} %copy-done.22) | copy-start | bytes 36868
  412.2 154.8 %reduce-scatter.16.cloned.1.call-start = ((), (), s32[]{:S(2)}) async-start(), calls=%async_computation.18 | async-start | bytes 3538944 | tf_op jit(solution)/shard_map/reduce_scatter | solution.py:196
  446.8 2.0 copy-start.17
  446.8 2.0 copy-start.21
  454.7 115.1 %reduce-scatter.22.cloned.1.call-start = ((), (), s32[]{:S(2)}) async-start(), calls=%async_computation.26 | async-start | bytes 1474560
  458.8 2.8 copy-start.10
  461.4 110.4 %all-reduce.6.cloned.1.call-start = ((), (), s32[]{:S(2)}) async-start(), calls=%async_computation.20 | async-start | bytes 1179648 | tf_op jit(solution)/shard_map/psum | solution.py:205
  461.6 7.0 copy-start.13
  461.6 7.0 copy-start.15
  461.6 7.0 copy-start.34
  468.6 10.6 %copy-start.9 = (bf16[1024,1536]{1,0:T(8,128)(2,1)S(1)}, bf16[1024,1536]{1,0:T(8,128)(2,1)}, u32[]{:S(2)}) copy-start(bf16[1024,1536]{1,0:T(8,128)(2,1)} %all-gather.17.cloned.1.call-done) | copy-start | bytes 9437188
  480.9 203.3 %reduce-scatter.20.cloned.1.call-start = ((), (), s32[]{:S(2)}) async-start(), calls=%async_computation.22 | async-start | bytes 21233664 | tf_op jit(solution)/shard_map/reduce_scatter | solution.py:160
  557.8 1.6 copy-start.11
  557.8 9.0 copy-start.6
  557.8 9.2 copy-start.19
  557.9 9.2 copy-start.28
  557.9 216.0 %reduce-scatter.12.cloned.1.call-start = ((), (), s32[]{:S(2)}) async-start(), calls=%async_computation.14 | async-start | bytes 1966080 | tf_op jit(solution)/shard_map/reduce_scatter | solution.py:167
  566.8 213.1 %reduce-scatter.18.cloned.1.call-start = ((), (), s32[]{:S(2)}) async-start(), calls=%async_computation.19 | async-start | bytes 184320 | tf_op jit(solution)/shard_map/reduce_scatter | solution.py:222
  569.7 238.7 %all-gather.25.cloned.1.call-start = ((), (), s32[]{:S(2)}) async-start(), calls=%async_computation.25 | async-start | bytes 2211840 | tf_op jit(solution)/shard_map/all_gather | solution.py:210
  571.7 277.7 %all-gather.19.cloned.1.call-start = ((), (), s32[]{:S(2)}) async-start(), calls=%async_computation.21 | async-start | bytes 5308416 | tf_op jit(solution)/shard_map/all_gather | solution.py:219
  572.4 378.2 %all-gather.21.cloned.1.call-start = ((), (), s32[]{:S(2)}) async-start(), calls=%async_computation.23 | async-start | bytes 21233664 | tf_op jit(solution)/shard_map/all_gather | solution.py:164
  771.9 1.9 copy-start.33
  771.9 2.0 copy-start.5
  771.9 2.0 copy-start.8
  771.9 2.0 copy-start.16
  771.9 2.0 copy-start.26
  771.9 2.0 copy-start.29
  772.0 2.0 copy-start.32
  984.0 29.1 %copy-start.1 = (bf16[384,1536]{1,0:T(8,128)(2,1)S(1)}, bf16[384,1536]{1,0:T(8,128)(2,1)}, u32[]{:S(2)}) copy-start(bf16[384,1536]{1,0:T(8,128)(2,1)} %param.15) | copy-start | bytes 3538948
Sparse Core Ops, SparseCore 0:
  28.4 33.5 all-gather.10
  85.3 46.5 reduce-scatter.9
  145.7 97.9 all-gather.22
  245.7 37.0 all-gather.12
  284.3 35.9 all-gather.14
  412.3 31.1 all-gather.16
  454.8 46.2 reduce-scatter.15
  503.4 35.9 reduce-scatter.21
  558.0 126.1 reduce-scatter.19
  686.9 60.2 reduce-scatter.11
  750.0 29.9 reduce-scatter.17
  782.4 26.0 all-gather.24
  810.5 38.8 all-gather.18
  851.9 98.7 all-gather.20
Sparse Core Ops, SparseCore 1:
  31.7 48.7 all-reduce.3
  375.2 33.5 reduce-scatter.13
  480.9 51.6 all-reduce.5
where the time goes:
time: 1030 us; the launch traced here: 1020 us
  waiting for transfers between devices  454 us (44%)
  blocking collectives  230 us (22%)
  local copies, waits for them, and re-layouts  154 us (15%)
  matrix products  89.6 us (9%)
  other arithmetic  70.9 us (7%)
  between operations  17.6 us (2%)
    reduce_scatter x1, waiting for transfers between devices, shards(): gw = lax.psum_scatter(gw, 'rep', scatter_dimension=0, tiled=True)  111 us
    all_gather x1, waiting for transfers between devices, shards(): gw = lax.all_gather(gw, 'rep', axis=0, tiled=True)  98.3 us
    all_gather x1, waiting for transfers between devices, shards(): both = lax.all_gather(both, 'rep', axis=0, tiled=False)  88.9 us
    all_to_all x1, blocking collectives, shards(): gw = lax.all_to_all(gw, 'grp', 0, 0, tiled=True)  84.3 us
    unnamed x85, local copies, waits for them, and re-layouts  72.8 us
    all_to_all x1, blocking collectives, shards(): both = lax.all_to_all(both, 'grp', 0, 0, tiled=True)  56 us
    reduce_scatter x1, waiting for transfers between devices, shards(): lax.psum_scatter(gact_part, 'grp', scatter_dimension=0, tiled=True)  33.6 us
    all_gather x1, waiting for transfers between devices, shards(): lax.all_gather(gres_low, 'rep', axis=0, tiled=True, axis_index_groups=gro...  31.3 us
  transfers between devices with their start and end apart: 18, of which 11 were waited for; matrix products, arithmetic and copies ran while one was open for 19% of the time, Pallas kernels for 0%

commit v1 on v0

--- a/solution.py
+++ b/solution.py
@@ -2,6 +2,7 @@
 import jax.numpy as jnp
 from jax import lax
 from jax.sharding import PartitionSpec as P
+from jax.lax import axis_index, axis_size, ppermute
 
 QUERY_HEADS = 24
 KEY_VALUE_HEADS = 8
@@ -14,6 +15,20 @@
 F32 = jnp.float32
 QPK = QUERY_HEADS // KEY_VALUE_HEADS
 BIG = 1 << 20
+
+
+def _note_lines(own_rows, dim_i, unit):
+    local_next = own_rows.shape
+    odd = own_rows.reshape(
+        *local_next[:dim_i], unit, local_next[dim_i] // unit, *local_next[dim_i + 1 :]
+    )
+    return jnp.moveaxis(odd, dim_i, 0)
+
+
+def _scan_core(my_data, which_dim):
+    my_data = jnp.moveaxis(my_data, 0, which_dim)
+    r2 = my_data.shape
+    return my_data.reshape(*r2[:which_dim], r2[which_dim] * r2[which_dim + 1], *r2[which_dim + 2 :])
 
 
 def dot(a, b):
@@ -159,7 +174,18 @@
     gw = gw.reshape(reps * grps * piece, EXPERTS // grps * 3 * HID)
     gw = lax.psum_scatter(gw, "rep", scatter_dimension=0, tiled=True)
     gw = gw.reshape(grps, piece, local_experts, 3 * HID)
-    gw = lax.all_to_all(gw, "grp", 0, 0, tiled=True)
+    shaped = axis_size("grp")
+    state_next = axis_index("grp")
+    x_now, reply = (shaped, state_next)
+    x_new = _note_lines(gw, 0, x_now)
+    cards = [x_new[reply]]
+    for hop_no in range(1, x_now):
+        field_out = x_new[reply ^ hop_no]
+        z_new = ppermute(field_out, "grp", [(nth, nth ^ hop_no) for nth in range(x_now)])
+        cards.append(z_new)
+    far_arr = jnp.stack(cards, 0)
+    x_new = far_arr[reply ^ jnp.arange(x_now)]
+    gw = _scan_core(x_new, 0)
     gw = gw.transpose(1, 0, 2, 3).reshape(piece, EXPERTS, 3 * HID)
     gw = lax.all_gather(gw, "rep", axis=0, tiled=True)
     grad_gu = gw[:, :, : 2 * HID].astype(F32)

time: 1030 us -> 991 us (0.962)
  blocking collectives: 230 us -> 146 us
  waiting for transfers between devices: 454 us -> 529 us
  local copies, waits for them, and re-layouts: 154 us -> 112 us
    all_to_all x1 -> x0, blocking collectives: 84.3 us -> none  [shards(): gw = lax.all_to_all(gw, 'grp', 0, 0, tiled=True)]
    ppermute x0 -> x3, waiting for transfers between devices: none -> 63.8 us  [shards(): ppermute(field_out, 'grp', [(nth, nth ^ hop_no) for nth in range(x_now)])]
    unnamed x85 -> x84, local copies, waits for them, and re-layouts: 72.8 us -> 27.1 us
  transfers between devices with their start and end apart: 18 -> 21, of which waited for: 11 -> 13; matrix products, arithmetic and copies ran while one was open for 19% -> 20% of each run, Pallas kernels for 0% -> 0%
where the time goes in v1:
time: 991 us; the launch traced here: 982 us
  waiting for transfers between devices  529 us (53%)
  blocking collectives  146 us (15%)
  local copies, waits for them, and re-layouts  112 us (11%)
  matrix products  89.7 us (9%)
  other arithmetic  78.2 us (8%)
  between operations  17.4 us (2%)
    reduce_scatter x1, waiting for transfers between devices, shards(): gw = lax.psum_scatter(gw, 'rep', scatter_dimension=0, tiled=True)  113 us
    all_gather x1, waiting for transfers between devices, shards(): gw = lax.all_gather(gw, 'rep', axis=0, tiled=True)  98.3 us
    all_gather x1, waiting for transfers between devices, shards(): both = lax.all_gather(both, 'rep', axis=0, tiled=False)  88.9 us
    ppermute x3, waiting for transfers between devices, shards(): ppermute(field_out, 'grp', [(nth, nth ^ hop_no) for nth in range(x_now)])  63.8 us
    all_to_all x1, blocking collectives, shards(): both = lax.all_to_all(both, 'grp', 0, 0, tiled=True)  56 us
    reduce_scatter x1, waiting for transfers between devices, shards(): lax.psum_scatter(gact_part, 'grp', scatter_dimension=0, tiled=True)  33.6 us
    all_gather x1, waiting for transfers between devices, shards(): lax.all_gather(gres_low, 'rep', axis=0, tiled=True, axis_index_groups=gro...  31.3 us
    all_gather x1, blocking collectives, shards(): qkv_head = lax.all_gather(qkv_cols, 'grp', axis=0, tiled=True)  30.3 us
  transfers between devices with their start and end apart: 21, of which 13 were waited for; matrix products, arithmetic and copies ran while one was open for 20% of the time, Pallas kernels for 0%

profile of v1, /device:TPU:0, one launch (start us, length us, event | category | flops | bytes accessed | tf_op | source)
XLA Modules:
  0.0 981.8 jit_solution(3075821671703443079)
XLA Ops:
  11.4 14.9 %all_gather.42 = bf16[1536,18]{0,1:T(8,128)(2,1)S(1)} all-gather(bf16[384,18]{0,1:T(8,128)(2,1)S(1)} %pad_maximum_fusion.17), channel_id=1, replica_groups=mesh['rep'=8,'grp'=4] {'grp'}, dimensions={0}, use_global_device_ids=true | all-gather | bytes 69120 | tf_op jit(solution)/shard_map/all_gather | solution.py:92
  26.3 1.9 fusion.50
  32.6 8.0 all-reduce
  43.2 30.3 %all_gather.44 = bf16[1536,320]{1,0:T(8,128)(2,1)S(1)} all-gather(bf16[384,320]{1,0:T(8,128)(2,1)S(1)} %pad_maximum_fusion.9), channel_id=1, replica_groups=mesh['rep'=8,'grp'=4] {'grp'}, dimensions={0}, use_global_device_ids=true | all-gather | bytes 1228800 | tf_op jit(solution)/shard_map/all_gather | solution.py:103
  73.8 3.1 convolution_bitcast_fusion
  77.5 1.9 fusion.105
  79.4 1.7 fusion.38
  81.4 3.7 convolution_convert_fusion.1
  86.4 1.5 constant_dynamic-slice_fusion.5
  88.2 1.3 copy.166
  89.5 56.0 %all_to_all.24 = bf16[4,4,48,1536]{3,2,1,0:T(8,128)(2,1)} all-to-all(bf16[4,4,48,1536]{3,2,1,0:T(8,128)(2,1)S(1)} %bitcast.210), channel_id=1, replica_groups=mesh['rep'=8,'grp'=4] {'grp'}, dimensions={0} | all-to-all | bytes 4718592 | tf_op jit(solution)/shard_map/all_to_all | solution.py:115
  146.9 1.9 multiply_convert_fusion.3
  150.9 2.5 convert_reduce_fusion
  154.7 88.9 %all-gather.23.cloned.1.call-done = bf16[32,4,48,1536]{3,2,1,0:T(8,128)(2,1)} async-done(((bf16[4,4,48,1536]{3,2,1,0:T(8,128)(2,1)}), bf16[32,4,48,1536]{3,2,1,0:T(8,128)(2,1)}) %all-gather.23.cloned.1.call-update) | async-done | bytes 18874384 | tf_op jit(solution)/shard_map/all_gather | solution.py:116
  243.6 17.1 %copy.167 = bf16[4,4,8,48,1536]{4,3,2,1,0:T(8,128)(2,1)} copy(bf16[4,4,8,48,1536]{4,3,0,1,2:T(8,128)(2,1)} %bitcast.205) | data formatting | bytes 37748736 | tf_op jit(solution)/shard_map/transpose | solution.py:117
  260.8 22.1 %all-gather.13.cloned.1.call-done = bf16[512,1536]{1,0:T(8,128)(2,1)} async-done(((bf16[128,1536]{1,0:T(8,128)(2,1)}), bf16[512,1536]{1,0:T(8,128)(2,1)}) %all-gather.13.cloned.1.call-update) | async-done | bytes 1572880 | tf_op jit(solution)/shard_map/all_gather | solution.py:150
  282.9 12.3 %fusion.18 = f32[4,512,1024]{1,2,0:T(8,128)} fusion(bf16[4,1536,1536]{2,1,0:T(8,128)(2,1)} %bitcast.201, bf16[512,1536]{1,0:T(8,128)(2,1)} %all-gather.13.cloned.1.call-done), kind=kOutput, calls=%fused_computation.32 | convolution fusion | flops 6442450944 | bytes 22544384 | tf_op jit(solution)/shard_map/td,edh->eth/dot_general | solution.py:153
  295.2 25.2 %all-gather.15.cloned.1.call-done = bf16[512,1536]{1,0:T(8,128)(2,1)} async-done(((bf16[128,1536]{1,0:T(8,128)(2,1)}), bf16[512,1536]{1,0:T(8,128)(2,1)}) %all-gather.15.cloned.1.call-update) | async-done | bytes 1572880 | tf_op jit(solution)/shard_map/all_gather | solution.py:149
  320.3 12.6 %fusion.10 = (f32[4,512]{1,0:T(4,128)}, f32[4,512,512]{2,1,0:T(8,128)}) fusion(f32[4,512,1024]{1,2,0:T(8,128)} %fusion.18, bf16[512,1536]{1,0:T(8,128)(2,1)} %all-gather.15.cloned.1.call-done, bf16[4,1536,1536]{2,1,0:T(8,128)(2,1)} %bitcast.202), kind=kOutput, calls=%fused_computation.20 | convolution fusion | flops 3228563456 | bytes 20455424 | tf_op jit(solution)/shard_map/td,edh->eth/dot_general | solution.py:159
  332.9 3.2 all-to-all-start.1
  336.3 5.5 all-to-all-done.1
  341.8 13.3 %all_gather.49 = f32[512,16]{0,1:T(8,128)S(1)} all-gather(f32[128,16]{0,1:T(8,128)S(1)} %get-tuple-element.84), channel_id=1, replica_groups=mesh['rep'=8,'grp'=4] {'grp'}, dimensions={0}, use_global_device_ids=true | all-gather | bytes 40960 | tf_op jit(solution)/shard_map/all_gather | solution.py:151
  355.1 6.9 multiply_convert_fusion.1
  362.1 1.4 copy-done.12
  364.1 10.8 %fusion.24 = bf16[512,1536]{1,0:T(8,128)(2,1)} fusion(bf16[4,1536,1536]{2,1,0:T(8,128)(2,1)} %bitcast.203, bf16[4,512,512]{1,2,0:T(8,128)(2,1)S(1)} %get-tuple-element.65, bf16[4,512,512]{1,2,0:T(8,128)(2,1)S(1)} %get-tuple-element.64), kind=kOutput, calls=%fused_computation.34 | convolution fusion | flops 6451625984 | bytes 18350080 | tf_op jit(solution)/shard_map/eth,edh->td/dot_general | solution.py:166
  375.0 33.6 %reduce-scatter.14.cloned.1.call-done = bf16[128,1536]{1,0:T(8,128)(2,1)} async-done(((bf16[512,1536]{1,0:T(8,128)(2,1)}), bf16[128,1536]{1,0:T(8,128)(2,1)}) %reduce-scatter.14.cloned.1.call-update) | async-done | bytes 393232 | tf_op jit(solution)/shard_map/reduce_scatter | solution.py:167
  408.5 1.5 multiply_reduce_fusion
  412.1 31.3 %all-gather.17.cloned.1.call-done = bf16[1024,1536]{1,0:T(8,128)(2,1)} async-done(((bf16[128,1536]{1,0:T(8,128)(2,1)}), bf16[1024,1536]{1,0:T(8,128)(2,1)}) %all-gather.17.cloned.1.call-update) | async-done | bytes 3145744 | tf_op jit(solution)/shard_map/all_gather | solution.py:207
  443.4 3.2 fusion.37
  446.7 2.0 fusion.46
  451.0 3.5 convolution_convert_fusion.2
  454.6 4.0 convolution_convert_fusion.3
  458.6 2.5 copy.205
  461.7 7.0 convert_bitcast_fusion
  468.7 10.6 %fusion.5 = bf16[4,1536,1024]{1,2,0:T(8,128)(2,1)} fusion(bf16[4,512,512]{1,2,0:T(8,128)(2,1)S(1)} %copy-done.15, bf16[4,512,512]{1,2,0:T(8,128)(2,1)S(1)} %copy-done.13, bf16[512,1536]{1,0:T(8,128)(2,1)S(1)} %copy-done.34), kind=kOutput, calls=%fused_computation.10 | convolution fusion | flops 6457131008 | bytes 18350080 | tf_op jit(solution)/shard_map/td,eth->edh/dot_general | solution.py:170
  479.3 1.6 convolution_convert_fusion.4
  481.0 20.9 %pad_maximum_fusion = bf16[4,1536,1536]{1,2,0:T(8,128)(2,1)} fusion(bf16[4,1536,512]{1,2,0:T(8,128)(2,1)} %convert_bitcast_fusion, bf16[4,1536,1024]{1,2,0:T(8,128)(2,1)} %fusion.5), kind=kLoop, calls=%fused_computation.3 | loop fusion | flops 37748736 | bytes 37748736 | tf_op jit(solution)/shard_map/concatenate | solution.py:172
  502.0 23.2 %copy.185 = bf16[4,1536,1536]{2,1,0:T(8,128)(2,1)} copy(bf16[4,1536,1536]{1,2,0:T(8,128)(2,1)} %pad_maximum_fusion) | data formatting | bytes 37748736 | tf_op jit(solution)/shard_map/concatenate | solution.py:172
  525.1 21.6 %copy.186 = bf16[8,4,48,4,1536]{4,3,2,1,0:T(4,128)(2,1)S(1)} copy(bf16[8,4,48,4,1536]{4,2,0,1,3:T(8,128)(2,1)} %bitcast.199) | data formatting | bytes 37748736 | tf_op jit(solution)/shard_map/transpose | solution.py:173
  546.7 9.7 copy.217
  556.5 1.5 copy-done.11
  558.0 7.4 fusion.21
  565.7 1.9 fusion.52
  568.4 1.9 copy.206
  571.2 112.9 %reduce-scatter.20.cloned.1.call-done = bf16[192,6144]{1,0:T(8,128)(2,1)} async-done(((bf16[1536,6144]{1,0:T(8,128)(2,1)}), bf16[192,6144]{1,0:T(8,128)(2,1)}) %reduce-scatter.20.cloned.1.call-update) | async-done | bytes 2359312 | tf_op jit(solution)/shard_map/reduce_scatter | solution.py:175
  684.2 3.5 reshape_reshape.3
  688.9 1.5 collective-permute-start
  690.4 2.4 collective-permute-start.1
  693.4 44.3 %collective-permute-done = bf16[1,48,4,1536]{3,1,2,0:T(8,128)(2,1)S(1)} collective-permute-done((bf16[1,48,4,1536]{3,1,2,0:T(8,128)(2,1)S(1)}, bf16[1,48,4,1536]{3,1,2,0:T(8,128)(2,1)S(1)}, u32[]{:S(2)}, u32[]{:S(2)}) %collective-permute-start) | collective-permute-done | bytes 589856 | tf_op jit(solution)/shard_map/ppermute | solution.py:184
  737.8 19.5 %collective-permute-done.1 = bf16[1,48,4,1536]{3,1,2,0:T(8,128)(2,1)S(1)} collective-permute-done((bf16[1,48,4,1536]{3,1,2,0:T(8,128)(2,1)S(1)}, bf16[1,48,4,1536]{3,1,2,0:T(8,128)(2,1)S(1)}, u32[]{:S(2)}, u32[]{:S(2)}) %collective-permute-start.1) | collective-permute-done | bytes 589856 | tf_op jit(solution)/shard_map/ppermute | solution.py:184
  757.6 2.1 gather_fusion.1
  759.7 4.5 copy.191
  764.3 2.6 fusion.49
  766.9 12.9 %reduce-scatter.18.cloned.1.call-done = f32[384,18]{0,1:T(8,128)} async-done(((f32[1536,18]{0,1:T(8,128)}), f32[384,18]{0,1:T(8,128)}) %reduce-scatter.18.cloned.1.call-update) | async-done | bytes 27664 | tf_op jit(solution)/shard_map/reduce_scatter | solution.py:248
  779.8 23.5 %psum.22 = f32[384,18]{0,1:T(8,128)S(1)} all-reduce(f32[384,18]{0,1:T(8,128)} %reduce-scatter.18.cloned.1.call-done), channel_id=1, replica_groups=mesh['rep'=8,'grp'=4] {'rep'}, use_global_device_ids=true, to_apply=%region_22.23 | all-reduce | flops 6912 | bytes 55296 | tf_op jit(solution)/shard_map/psum | solution.py:248
  804.5 3.8 all-gather.25.cloned.1.call-done
  808.3 2.0 convert_element_type.169
  812.1 2.2 pad_maximum_fusion.2
  814.3 5.5 copy.192
  819.8 29.4 %all-gather.19.cloned.1.call-done = bf16[1536,1536]{1,0:T(8,128)(2,1)} async-done(((bf16[192,1536]{1,0:T(8,128)(2,1)}), bf16[1536,1536]{1,0:T(8,128)(2,1)}) %all-gather.19.cloned.1.call-update) | async-done | bytes 4718608 | tf_op jit(solution)/shard_map/all_gather | solution.py:245
  849.2 3.0 dynamic-slice_convert_fusion
  852.2 98.3 %all-gather.21.cloned.1.call-done = bf16[384,16,1536]{2,1,0:T(8,128)(2,1)} async-done(((bf16[48,16,1536]{2,1,0:T(8,128)(2,1)}), bf16[384,16,1536]{2,1,0:T(8,128)(2,1)}) %all-gather.21.cloned.1.call-update) | async-done | bytes 18874384 | tf_op jit(solution)/shard_map/all_gather | solution.py:190
  950.5 9.3 slice_convert_fusion.1
  959.8 14.4 %slice_convert_fusion = f32[384,16,1024]{2,1,0:T(8,128)} fusion(bf16[384,16,1536]{2,1,0:T(8,128)(2,1)} %all-gather.21.cloned.1.call-done), kind=kLoop, calls=%fused_computation.5 | loop fusion | flops 6291456 | bytes 37748736 | tf_op jit(solution)/shard_map/convert_element_type | solution.py:191
  (189 shorter events, 29.6 us)
Async XLA Ops:
  8.0 20.4 %copy-start = (bf16[384,1536]{1,0:T(8,128)(2,1)S(1)}, bf16[384,1536]{1,0:T(8,128)(2,1)}, u32[]{:S(2)}) copy-start(bf16[384,1536]{1,0:T(8,128)(2,1)} %param.15) | copy-start | bytes 3538948
  8.0 65.7 %all-gather.11.cloned.1.call-start = ((), (), s32[]{:S(2)}) async-start(), calls=%async_computation.9 | async-start | bytes 3538944 | tf_op jit(solution)/shard_map/all_gather | solution.py:123
  9.3 19.0 %copy-start.27 = (f32[128]{0:T(128)}, f32[128]{0:T(128)S(1)}, u32[]{:S(2)}) copy-start(f32[128]{0:T(128)S(1)} %add_rsqrt_fusion.1) | copy-start | bytes 1540
  26.3 3.2 copy-start.18
  28.3 53.1 %all-reduce.4.cloned.1.call-start = ((), (), s32[]{:S(2)}) async-start(), calls=%async_computation.10 | async-start | bytes 1179648 | tf_op jit(solution)/shard_map/psum | solution.py:109
  28.4 2.9 copy-start.35
  30.5 115.1 %reduce-scatter.10.cloned.1.call-start = ((), (), s32[]{:S(2)}) async-start(), calls=%async_computation.11 | async-start | bytes 3538944 | tf_op jit(solution)/shard_map/reduce_scatter | solution.py:143
  77.5 3.6 copy-start.20
  79.4 2.0 copy-start.22
  85.2 158.4 %all-gather.23.cloned.1.call-start = ((), (), s32[]{:S(2)}) async-start(), calls=%async_computation.23 | async-start | bytes 21233664 | tf_op jit(solution)/shard_map/all_gather | solution.py:116
  89.5 56.1 %copy-start.2 = (bf16[128,1536]{1,0:T(8,128)(2,1)S(1)}, bf16[128,1536]{1,0:T(8,128)(2,1)}, u32[]{:S(2)}) copy-start(bf16[128,1536]{1,0:T(8,128)(2,1)} %param.12) | copy-start | bytes 1179652
  145.5 3.9 copy-start.24
  145.5 4.4 copy-start.30
  145.6 137.3 %all-gather.13.cloned.1.call-start = ((), (), s32[]{:S(2)}) async-start(), calls=%async_computation.12 | async-start | bytes 1966080 | tf_op jit(solution)/shard_map/all_gather | solution.py:150
  146.9 263.2 %copy-start.25 = (f32[128]{0:T(128)}, f32[128]{0:T(128)S(1)}, u32[]{:S(2)}) copy-start(f32[128]{0:T(128)S(1)} %add_rsqrt_fusion) | copy-start | bytes 1540
  148.8 171.5 %all-gather.15.cloned.1.call-start = ((), (), s32[]{:S(2)}) async-start(), calls=%async_computation.14 | async-start | bytes 1966080 | tf_op jit(solution)/shard_map/all_gather | solution.py:149
  332.9 8.8 all-to-all-start.1
  336.2 72.4 %reduce-scatter.14.cloned.1.call-start = ((), (), s32[]{:S(2)}) async-start(), calls=%async_computation.15 | async-start | bytes 1966080 | tf_op jit(solution)/shard_map/reduce_scatter | solution.py:167
  362.1 1.4 copy-start.12
  362.1 2.0 copy-start.14
  364.1 44.5 %copy-start.3 = (bf16[128,1536]{1,0:T(8,128)(2,1)S(1)}, bf16[128,1536]{1,0:T(8,128)(2,1)}, u32[]{:S(2)}) copy-start(bf16[128,1536]{1,0:T(8,128)(2,1)} %reduce-scatter.10.cloned.1.call-done) | copy-start | bytes 1179652
  374.9 36.0 %copy-start.7 = (bf16[128,1536]{1,0:T(8,128)(2,1)S(1)}, bf16[128,1536]{1,0:T(8,128)(2,1)}, u32[]{:S(2)}) copy-start(bf16[128,1536]{1,0:T(8,128)(2,1)} %param.23) | copy-start | bytes 1179652
  374.9 68.5 %all-gather.17.cloned.1.call-start = ((), (), s32[]{:S(2)}) async-start(), calls=%async_computation.16 | async-start | bytes 3538944 | tf_op jit(solution)/shard_map/all_gather | solution.py:207
  410.0 0.9 copy-start.4
  410.1 36.5 %copy-start.31 = (f32[128]{0:T(128)}, f32[128]{0:T(128)S(1)}, u32[]{:S(2)}) copy-start(f32[128]{0:T(128)S(1)} %broadcast_multiply_fusion.1) | copy-start | bytes 1540
  412.0 34.6 %copy-start.23 = (f32[8,3,128]{2,1,0:T(4,128)S(1)}, f32[8,3,128]{2,1,0:T(4,128)}, u32[]{:S(2)}) copy-start(f32[8,3,128]{2,1,0:T(4,128)} %copy-done.22) | copy-start | bytes 36868
  412.1 153.6 %reduce-scatter.16.cloned.1.call-start = ((), (), s32[]{:S(2)}) async-start(), calls=%async_computation.17 | async-start | bytes 3538944 | tf_op jit(solution)/shard_map/reduce_scatter | solution.py:222
  446.7 2.0 copy-start.17
  446.7 2.0 copy-start.21
  454.5 113.8 %reduce-scatter.22.cloned.1.call-start = ((), (), s32[]{:S(2)}) async-start(), calls=%async_computation.25 | async-start | bytes 1474560
  458.6 3.0 copy-start.10
  461.2 109.1 %all-reduce.6.cloned.1.call-start = ((), (), s32[]{:S(2)}) async-start(), calls=%async_computation.19 | async-start | bytes 1179648 | tf_op jit(solution)/shard_map/psum | solution.py:231
  461.7 7.1 copy-start.13
  461.7 7.0 copy-start.15
  461.7 7.0 copy-start.34
  468.7 10.6 %copy-start.9 = (bf16[1024,1536]{1,0:T(8,128)(2,1)S(1)}, bf16[1024,1536]{1,0:T(8,128)(2,1)}, u32[]{:S(2)}) copy-start(bf16[1024,1536]{1,0:T(8,128)(2,1)} %all-gather.17.cloned.1.call-done) | copy-start | bytes 9437188
  481.0 203.2 %reduce-scatter.20.cloned.1.call-start = ((), (), s32[]{:S(2)}) async-start(), calls=%async_computation.21 | async-start | bytes 21233664 | tf_op jit(solution)/shard_map/reduce_scatter | solution.py:175
  556.4 1.6 copy-start.11
  556.4 9.0 copy-start.6
  556.4 9.2 copy-start.19
  556.4 9.2 copy-start.28
  556.4 207.8 %reduce-scatter.12.cloned.1.call-start = ((), (), s32[]{:S(2)}) async-start(), calls=%async_computation.13 | async-start | bytes 1966080 | tf_op jit(solution)/shard_map/reduce_scatter | solution.py:193
  565.4 214.4 %reduce-scatter.18.cloned.1.call-start = ((), (), s32[]{:S(2)}) async-start(), calls=%async_computation.18 | async-start | bytes 184320 | tf_op jit(solution)/shard_map/reduce_scatter | solution.py:248
  568.3 240.0 %all-gather.25.cloned.1.call-start = ((), (), s32[]{:S(2)}) async-start(), calls=%async_computation.24 | async-start | bytes 2211840 | tf_op jit(solution)/shard_map/all_gather | solution.py:236
  570.3 279.0 %all-gather.19.cloned.1.call-start = ((), (), s32[]{:S(2)}) async-start(), calls=%async_computation.20 | async-start | bytes 5308416 | tf_op jit(solution)/shard_map/all_gather | solution.py:245
  571.0 379.5 %all-gather.21.cloned.1.call-start = ((), (), s32[]{:S(2)}) async-start(), calls=%async_computation.22 | async-start | bytes 21233664 | tf_op jit(solution)/shard_map/all_gather | solution.py:190
  688.9 48.9 %collective-permute-start = (bf16[1,48,4,1536]{3,1,2,0:T(8,128)(2,1)S(1)}, bf16[1,48,4,1536]{3,1,2,0:T(8,128)(2,1)S(1)}, u32[]{:S(2)}, u32[]{:S(2)}) collective-permute-start(bf16[1,48,4,1536]{3,1,2,0:T(8,128)(2,1)S(1)} %bitcast.225), channel_id=1, source_target_pairs={{0,1},{1,0},{2,3},{3,2},{4,5},{5,4},{6,7},{7,6},{8,9},{9,8},{10,11... | collective-permute-start | bytes 1769480 | tf_op jit(solution)/shard_map/ppermute | solution.py:184
  690.4 66.9 %collective-permute-start.1 = (bf16[1,48,4,1536]{3,1,2,0:T(8,128)(2,1)S(1)}, bf16[1,48,4,1536]{3,1,2,0:T(8,128)(2,1)S(1)}, u32[]{:S(2)}, u32[]{:S(2)}) collective-permute-start(bf16[1,48,4,1536]{3,1,2,0:T(8,128)(2,1)S(1)} %bitcast.224), channel_id=1, source_target_pairs={{0,2},{1,3},{2,0},{3,1},{4,6},{5,7},{6,4},{7,5},{8,10},{9,11},{10,... | collective-permute-start | bytes 1769480 | tf_op jit(solution)/shard_map/ppermute | solution.py:184
  692.8 64.5 %collective-permute-start.2 = (bf16[1,48,4,1536]{3,1,2,0:T(8,128)(2,1)S(1)}, bf16[1,48,4,1536]{3,1,2,0:T(8,128)(2,1)S(1)}, u32[]{:S(2)}, u32[]{:S(2)}) collective-permute-start(bf16[1,48,4,1536]{3,1,2,0:T(8,128)(2,1)S(1)} %bitcast.223), channel_id=1, source_target_pairs={{0,3},{1,2},{2,1},{3,0},{4,7},{5,6},{6,5},{7,4},{8,11},{9,10},{10,... | collective-permute-start | bytes 1769480 | tf_op jit(solution)/shard_map/ppermute | solution.py:184
  759.7 4.6 copy-start.33
  759.7 4.6 copy-start.5
  759.7 4.6 copy-start.8
  759.7 4.6 copy-start.16
  759.7 4.6 copy-start.26
  759.7 4.6 copy-start.29
  759.7 4.6 copy-start.32
  959.8 14.4 %copy-start.1 = (bf16[384,1536]{1,0:T(8,128)(2,1)S(1)}, bf16[384,1536]{1,0:T(8,128)(2,1)}, u32[]{:S(2)}) copy-start(bf16[384,1536]{1,0:T(8,128)(2,1)} %param.15) | copy-start | bytes 3538948
Sparse Core Ops, SparseCore 0:
  28.4 33.5 all-gather.10
  85.3 46.4 reduce-scatter.9
  145.7 97.9 all-gather.22
  245.7 37.0 all-gather.12
  284.3 35.9 all-gather.14
  412.2 31.1 all-gather.16
  454.7 46.2 reduce-scatter.15
  503.3 36.3 reduce-scatter.21
  556.5 127.6 reduce-scatter.19
  686.9 59.3 reduce-scatter.11
  748.6 31.1 reduce-scatter.17
  782.3 25.9 all-gather.24
  810.3 38.8 all-gather.18
  851.7 98.7 all-gather.20
Sparse Core Ops, SparseCore 1:
  31.7 48.7 all-reduce.3
  375.0 33.5 reduce-scatter.13
  481.1 51.5 all-reduce.5
